TPU v7x, 32 devices: a whole 2x2x4 slice. The times are simulated.
32 devices in a mesh: groups: 2 (over x), tm: 8 (over z, y), mp: 2 (over core).
Axes of the slice: x: 2, y: 2, z: 4, core: 2. Of those that a mesh axis runs over, the one named last changes fastest.
Arguments:
- branch_x: bfloat16 [8192, 4096], P(('groups', 'tm'), 'mp'), parts along dimension 0, may hold values from -6 to 6
- branch_y: bfloat16 [8192, 4096], P(('groups', 'tm'), 'mp'), parts along dimension 0, may hold values from -6 to 6
- queries: bfloat16 [8192, 4096], P(('groups', 'tm'), 'mp'), parts along dimension 0, may hold values from -1500 to 1500
- conv_weight: float32 [4, 4096], P(None, 'mp'), may hold values from -3 to 3
- conv_bias: float32 [4096], P('mp'), may hold values from -3 to 3
- gate_panel: bfloat16 [16, 256, 512], P('mp'), may hold values from -0.375 to 0.375
- gate_scale: float32 [16, 2, 512], P('mp'), may hold values from 0.5 to 2
- gate_bias: float32 [2, 4096], P(None, 'mp'), may hold values from -4 to 4
- decay_rate: float32 [4096], P('mp'), may hold values from 2.4414063e-05 to 0.05
- kv_panel: bfloat16 [4096, 512], P('mp'), may hold values from -0.09375 to 0.09375
- kv_scale: float32 [32, 512], P('mp'), may hold values from 0.5 to 2
- segment_ids: int32 [8192], P('groups'), parts along dimension 0, may hold values from 0 to 3, never falling along the last dimension, each value on 1 to 2048 neighbouring positions
Outputs:
- mixed: bfloat16 [8192, 4096], P(('groups', 'tm'), 'mp'), parts along dimension 0
- attended: bfloat16 [8192, 4096], P(('groups', 'tm'), 'mp'), parts along dimension 0
There are 2 independent parts, one for each index of `groups`. A program takes and returns all parts, laid end to end along the dimension named above; an argument that names none is the same for every part. Nothing has to cross between parts.
Inputs may be any that keep to these rules, and one draw needn't show every extreme that they name: `segment_ids`: never falls along the sequence; each of the 4 documents holds 1 to 2048 positions, one of them exactly 2048.
All inputs are finite; a program needn't handle non-finite values.
Results may differ from a plain program's by a relative error of at most 0.03.
Values may be sent and summed in bfloat16 or wider, within the bound.
A program may use at most 128 MiB of HBM per device.

v0:
```python
import math

import jax
import jax.numpy as jnp
from jax import lax
from jax.sharding import PartitionSpec as P

HD = 256
CONV = 4
WINDOW = 2048
SCALE_ROWS = 128


def from_behind(block, axis, distance):
    devices = range(lax.axis_size(axis))
    route = [(i - distance, i) for i in devices if i - distance in devices]
    return lax.ppermute(block, axis, route)


def dequantize(weight_panel, scales):
    row_count = weight_panel.shape[-2]
    shaped = weight_panel.astype(jnp.float32).reshape(
        weight_panel.shape[:-2] + (row_count // SCALE_ROWS, SCALE_ROWS, weight_panel.shape[-1])
    )
    return (shaped * jnp.expand_dims(scales, -2)).reshape(weight_panel.shape).astype(jnp.bfloat16)


def compose(earlier, follow):
    return (earlier[0] * follow[0], follow[0] * earlier[1] + follow[1])


def local_recurrence(decay, scaled_input):
    local_tokens = decay.shape[0]
    channels = decay.shape[1]
    group_len = math.gcd(local_tokens, 16)
    group_count = local_tokens // group_len
    decay_groups = decay.reshape(group_count, group_len, channels)
    input_groups = scaled_input.reshape(group_count, group_len, channels)

    def within(row_index, carry):
        run_prod, run_state, prod_buffer, state_buffer = carry
        decay_row = lax.dynamic_slice_in_dim(decay_groups, row_index, 1, 1)
        input_row = lax.dynamic_slice_in_dim(input_groups, row_index, 1, 1)
        run_prod = run_prod * decay_row
        run_state = decay_row * run_state + input_row
        prod_buffer = lax.dynamic_update_slice_in_dim(prod_buffer, run_prod, row_index, 1)
        state_buffer = lax.dynamic_update_slice_in_dim(state_buffer, run_state, row_index, 1)
        return (run_prod, run_state, prod_buffer, state_buffer)

    start_prod = jnp.ones((group_count, 1, channels), jnp.float32)
    start_state = jnp.zeros((group_count, 1, channels), jnp.float32)
    empty_buffer = jnp.zeros((group_count, group_len, channels), jnp.float32)
    group_prod, group_state, prod_buffer, state_buffer = lax.fori_loop(
        0, group_len, within, (start_prod, start_state, empty_buffer, empty_buffer)
    )

    def across(carry, pair):
        entering_prod, entering_state = carry
        return (compose(carry, pair), (entering_prod, entering_state))

    start_pair = (jnp.ones((channels,), jnp.float32), jnp.zeros((channels,), jnp.float32))
    final_pair, entering = lax.scan(across, start_pair, (group_prod[:, 0, :], group_state[:, 0, :]))
    decay_prod = (prod_buffer * entering[0][:, None, :]).reshape(local_tokens, channels)
    local_state = (state_buffer + prod_buffer * entering[1][:, None, :]).reshape(
        local_tokens, channels
    )
    return (decay_prod, local_state, final_pair[0], final_pair[1])


def attend_block(query_block, key_block, value_block, allowed):
    scores = jnp.einsum(
        "td,sd->ts", query_block, key_block, preferred_element_type=jnp.float32
    ) * HD ** (-0.5)
    scores = jnp.where(allowed, scores, jnp.float32(-1e30))
    highest = jnp.max(scores, axis=-1, keepdims=True)
    weights_raw = jnp.exp(scores - highest) * allowed.astype(jnp.float32)
    totals = jnp.sum(weights_raw, axis=-1, keepdims=True)
    weights = (weights_raw / totals).astype(jnp.bfloat16)
    return jnp.dot(weights, value_block, preferred_element_type=jnp.float32).astype(jnp.bfloat16)


def earlier_keys(block, window_blocks):
    earlier_blocks = []
    for lag_index in range(1, window_blocks + 1):
        earlier_blocks.append(from_behind(block, "tm", lag_index))
    return earlier_blocks[::-1] + [block]


def local(
    branch_x,
    branch_y,
    queries,
    conv_weight,
    conv_bias,
    gate_panel,
    gate_scale,
    gate_bias,
    decay_rate,
    kv_panel,
    kv_scale,
    segment_ids,
):
    local_tokens = branch_x.shape[0]
    channels = branch_x.shape[1]
    block_count = gate_panel.shape[0]
    block_width = gate_panel.shape[1]
    head_count = queries.shape[1] // HD
    first_row = lax.axis_index("tm") * local_tokens
    padded_ids = jnp.concatenate([-jnp.ones((WINDOW,), jnp.int32), segment_ids])
    near_ids = lax.dynamic_slice_in_dim(
        padded_ids, first_row + (WINDOW - CONV + 1), local_tokens + CONV - 1
    )
    own_ids = near_ids[CONV - 1 :]
    resets = own_ids != near_ids[CONV - 2 : CONV - 2 + local_tokens]
    carried = from_behind(branch_x[local_tokens - CONV + 1 :], "tm", 1)
    extended = jnp.concatenate([carried, branch_x], 0)
    conv_sum = jnp.zeros((local_tokens, channels), jnp.float32)
    for lag_index in range(CONV):
        offset = CONV - 1 - lag_index
        same_doc = (near_ids[offset : offset + local_tokens] == own_ids).astype(jnp.float32)
        conv_sum = (
            conv_sum
            + conv_weight[lag_index]
            * extended[offset : offset + local_tokens].astype(jnp.float32)
            * same_doc[:, None]
        )
    conv_out = (conv_sum + conv_bias).astype(jnp.bfloat16)
    gate_weight = dequantize(gate_panel, gate_scale)
    gate_pre = jnp.einsum(
        "tbi,bio->tbo",
        conv_out.reshape(local_tokens, block_count, block_width),
        gate_weight,
        preferred_element_type=jnp.float32,
    )
    recur_gate = jax.nn.sigmoid(
        gate_pre[..., :block_width].reshape(local_tokens, channels) + gate_bias[0]
    )
    input_gate = jax.nn.sigmoid(
        gate_pre[..., block_width:].reshape(local_tokens, channels) + gate_bias[1]
    )
    log_decay = -8.0 * recur_gate * decay_rate
    decay = jnp.where(resets[:, None], jnp.float32(0.0), jnp.exp(log_decay))
    normalizer = jnp.where(resets[:, None], jnp.float32(1.0), jnp.sqrt(-jnp.expm1(2.0 * log_decay)))
    scaled_input = input_gate * conv_out.astype(jnp.float32) * normalizer
    decay_prod, local_state, prod_end, state_end = local_recurrence(decay, scaled_input)

    def relay_state(step_index, incoming_state):
        return from_behind(prod_end * incoming_state + state_end, "tm", 1)

    incoming = lax.fori_loop(0, lax.axis_size("tm") - 1, relay_state, jnp.zeros_like(state_end))
    state = local_state + decay_prod * incoming[None, :]
    mixed = (state * jax.nn.gelu(branch_y.astype(jnp.float32), approximate=True)).astype(
        jnp.bfloat16
    )
    partial_kv = jnp.dot(mixed, dequantize(kv_panel, kv_scale), preferred_element_type=jnp.float32)
    window_blocks = WINDOW // local_tokens
    keys_values = lax.psum(partial_kv, "mp").astype(jnp.bfloat16)
    ordered = jnp.concatenate(earlier_keys(keys_values, window_blocks), 0)
    all_keys = ordered[:, :HD]
    all_values = ordered[:, HD:]
    key_ids = lax.dynamic_slice_in_dim(padded_ids, first_row, WINDOW + local_tokens)
    key_pos = first_row - WINDOW + jnp.arange(WINDOW + local_tokens, dtype=jnp.int32)
    query_pos = first_row + jnp.arange(local_tokens, dtype=jnp.int32)
    allowed = (
        (key_pos[None, :] <= query_pos[:, None])
        & (query_pos[:, None] - key_pos[None, :] < WINDOW)
        & (key_ids[None, :] == own_ids[:, None])
    )

    def one_head(head_index, attended_now):
        column = head_index * HD
        query_block = lax.dynamic_slice_in_dim(queries, column, HD, 1)
        head_result = attend_block(query_block, all_keys, all_values, allowed)
        return lax.dynamic_update_slice_in_dim(attended_now, head_result, column, 1)

    attended = lax.fori_loop(
        0, head_count, one_head, jnp.zeros((local_tokens, head_count * HD), jnp.bfloat16)
    )
    return (mixed, attended)


def solution(mesh):
    in_specs = (
        P(("groups", "tm"), "mp"),
        P(("groups", "tm"), "mp"),
        P(("groups", "tm"), "mp"),
        P(None, "mp"),
        P("mp"),
        P("mp", None, None),
        P("mp", None, None),
        P(None, "mp"),
        P("mp"),
        P("mp", None),
        P("mp", None),
        P("groups"),
    )
    out_specs = (P(("groups", "tm"), "mp"), P(("groups", "tm"), "mp"))
    return jax.shard_map(local, mesh=mesh, in_specs=in_specs, out_specs=out_specs, check_vma=False)
```

profile of v0, /device:TPU:16, one launch (start us, length us, event | category | flops | bytes accessed | tf_op | source)
XLA Modules:
  0.0 521.5 jit_solution(16822371875046340460)
XLA Ops:
  42.7 6.1 %exponential_select_fusion.1 = f32[32,16,2048]{2,1,0:T(8,128)} fusion(f32[32,16,2048]{2,1,0:T(8,128)} %reshape.73, f32[2048]{0:T(1024)S(1)} %broadcast_multiply_fusion.1, f32[2048]{0:T(1024)S(1)} %bitcast.70, pred[32,16]{1,0:T(8,128)(4,1)S(1)} %ne.8), kind=kLoop, calls=%fused_computation.44 | loop fusion | flops 6291456 | bytes 8405504 | tf_op jit(solution)/shard_map/jit(_where)/select_n | solution.py:142
  48.9 6.1 %select_multiply_fusion = f32[512,2048]{1,0:T(8,128)} fusion(f32[512,2048]{1,0:T(8,128)S(1)} %copy-done, bf16[512,2048]{1,0:T(8,128)(2,1)S(1)} %add_convert_fusion, f32[512,2048]{1,0:T(8,128)S(1)} %copy-done.1, f32[2048]{0:T(1024)S(1)} %broadcast_multiply_fusion.1, f32[2048]{0:T(1024)S(1)} %bitcast.71, f32[2048]{0:T(1024)S(1)} %bitcast.72, ...), kind=kLoop, calls=%fused_computation.43 | loop fusion | flops 15728640 | bytes 14705152 | tf_op jit(solution)/shard_map/mul | solution.py:144
  55.0 241.5 %while.67 = (s32[]{:T(128)}, f32[32,1,2048]{2,1,0:T(1,128)S(1)}, f32[32,1,2048]{2,1,0:T(1,128)S(1)}, f32[32,16,2048]{2,1,0:T(8,128)}, f32[32,16,2048]{2,1,0:T(8,...) while((s32[]{:T(128)}, f32[32,1,2048]{2,1,0:T(1,128)S(1)}, ...), condition=%wide.region_1.2_spmd.clone.clone, body=%wide.region_0.1_spmd.clone.sunk.clone | while | flops 327683 | bytes 2621539 | solution.py:53
  178.6 6.0 %dynamic_update_slice.45 = f32[32,16,2048]{2,1,0:T(8,128)} dynamic-update-slice(f32[32,16,2048]{2,1,0:T(8,128)} %get-tuple-element.741, f32[32,1,2048]{2,1,0:T(1,128)S(1)} %get-tuple-element.746, s32[]{:T(128)} %constant.122.clone.1..sunk.4, s32[]{:T(128)} %get-tuple-element.738, s32[]{:T(128)} %constant.122.clone.1..sunk.4) | dynamic-update-slice | bytes 524292 | tf_op jit(solution)/shard_map/while/body/eval_jaxpr/dynamic_update_slice | solution.py:46
  184.6 6.0 %dynamic_update_slice.46 = f32[32,16,2048]{2,1,0:T(8,128)} dynamic-update-slice(f32[32,16,2048]{2,1,0:T(8,128)} %get-tuple-element.742, f32[32,1,2048]{2,1,0:T(1,128)S(1)} %get-tuple-element.747, s32[]{:T(128)} %constant.122.clone.1..sunk.4, s32[]{:T(128)} %get-tuple-element.738, s32[]{:T(128)} %constant.122.clone.1..sunk.4) | dynamic-update-slice | bytes 524292 | tf_op jit(solution)/shard_map/while/body/eval_jaxpr/dynamic_update_slice | solution.py:47
  193.7 6.0 %dynamic_update_slice.45 = f32[32,16,2048]{2,1,0:T(8,128)} dynamic-update-slice(f32[32,16,2048]{2,1,0:T(8,128)} %get-tuple-element.741, f32[32,1,2048]{2,1,0:T(1,128)S(1)} %get-tuple-element.746, s32[]{:T(128)} %constant.122.clone.1..sunk.4, s32[]{:T(128)} %get-tuple-element.738, s32[]{:T(128)} %constant.122.clone.1..sunk.4) | dynamic-update-slice | bytes 524292 | tf_op jit(solution)/shard_map/while/body/eval_jaxpr/dynamic_update_slice | solution.py:46
  199.7 6.0 %dynamic_update_slice.46 = f32[32,16,2048]{2,1,0:T(8,128)} dynamic-update-slice(f32[32,16,2048]{2,1,0:T(8,128)} %get-tuple-element.742, f32[32,1,2048]{2,1,0:T(1,128)S(1)} %get-tuple-element.747, s32[]{:T(128)} %constant.122.clone.1..sunk.4, s32[]{:T(128)} %get-tuple-element.738, s32[]{:T(128)} %constant.122.clone.1..sunk.4) | dynamic-update-slice | bytes 524292 | tf_op jit(solution)/shard_map/while/body/eval_jaxpr/dynamic_update_slice | solution.py:47
  214.9 6.0 %dynamic_update_slice.46 = f32[32,16,2048]{2,1,0:T(8,128)} dynamic-update-slice(f32[32,16,2048]{2,1,0:T(8,128)} %get-tuple-element.742, f32[32,1,2048]{2,1,0:T(1,128)S(1)} %get-tuple-element.747, s32[]{:T(128)} %constant.122.clone.1..sunk.4, s32[]{:T(128)} %get-tuple-element.738, s32[]{:T(128)} %constant.122.clone.1..sunk.4) | dynamic-update-slice | bytes 524292 | tf_op jit(solution)/shard_map/while/body/eval_jaxpr/dynamic_update_slice | solution.py:47
  230.0 6.0 %dynamic_update_slice.46 = f32[32,16,2048]{2,1,0:T(8,128)} dynamic-update-slice(f32[32,16,2048]{2,1,0:T(8,128)} %get-tuple-element.742, f32[32,1,2048]{2,1,0:T(1,128)S(1)} %get-tuple-element.747, s32[]{:T(128)} %constant.122.clone.1..sunk.4, s32[]{:T(128)} %get-tuple-element.738, s32[]{:T(128)} %constant.122.clone.1..sunk.4) | dynamic-update-slice | bytes 524292 | tf_op jit(solution)/shard_map/while/body/eval_jaxpr/dynamic_update_slice | solution.py:47
  239.1 6.0 %dynamic_update_slice.45 = f32[32,16,2048]{2,1,0:T(8,128)} dynamic-update-slice(f32[32,16,2048]{2,1,0:T(8,128)} %get-tuple-element.741, f32[32,1,2048]{2,1,0:T(1,128)S(1)} %get-tuple-element.746, s32[]{:T(128)} %constant.122.clone.1..sunk.4, s32[]{:T(128)} %get-tuple-element.738, s32[]{:T(128)} %constant.122.clone.1..sunk.4) | dynamic-update-slice | bytes 524292 | tf_op jit(solution)/shard_map/while/body/eval_jaxpr/dynamic_update_slice | solution.py:46
  245.1 6.0 %dynamic_update_slice.46 = f32[32,16,2048]{2,1,0:T(8,128)} dynamic-update-slice(f32[32,16,2048]{2,1,0:T(8,128)} %get-tuple-element.742, f32[32,1,2048]{2,1,0:T(1,128)S(1)} %get-tuple-element.747, s32[]{:T(128)} %constant.122.clone.1..sunk.4, s32[]{:T(128)} %get-tuple-element.738, s32[]{:T(128)} %constant.122.clone.1..sunk.4) | dynamic-update-slice | bytes 524292 | tf_op jit(solution)/shard_map/while/body/eval_jaxpr/dynamic_update_slice | solution.py:47
  254.2 6.0 %dynamic_update_slice.45 = f32[32,16,2048]{2,1,0:T(8,128)} dynamic-update-slice(f32[32,16,2048]{2,1,0:T(8,128)} %get-tuple-element.741, f32[32,1,2048]{2,1,0:T(1,128)S(1)} %get-tuple-element.746, s32[]{:T(128)} %constant.122.clone.1..sunk.4, s32[]{:T(128)} %get-tuple-element.738, s32[]{:T(128)} %constant.122.clone.1..sunk.4) | dynamic-update-slice | bytes 524292 | tf_op jit(solution)/shard_map/while/body/eval_jaxpr/dynamic_update_slice | solution.py:46
  260.2 6.0 %dynamic_update_slice.46 = f32[32,16,2048]{2,1,0:T(8,128)} dynamic-update-slice(f32[32,16,2048]{2,1,0:T(8,128)} %get-tuple-element.742, f32[32,1,2048]{2,1,0:T(1,128)S(1)} %get-tuple-element.747, s32[]{:T(128)} %constant.122.clone.1..sunk.4, s32[]{:T(128)} %get-tuple-element.738, s32[]{:T(128)} %constant.122.clone.1..sunk.4) | dynamic-update-slice | bytes 524292 | tf_op jit(solution)/shard_map/while/body/eval_jaxpr/dynamic_update_slice | solution.py:47
  275.3 6.0 %dynamic_update_slice.46 = f32[32,16,2048]{2,1,0:T(8,128)} dynamic-update-slice(f32[32,16,2048]{2,1,0:T(8,128)} %get-tuple-element.742, f32[32,1,2048]{2,1,0:T(1,128)S(1)} %get-tuple-element.747, s32[]{:T(128)} %constant.122.clone.1..sunk.4, s32[]{:T(128)} %get-tuple-element.738, s32[]{:T(128)} %constant.122.clone.1..sunk.4) | dynamic-update-slice | bytes 524292 | tf_op jit(solution)/shard_map/while/body/eval_jaxpr/dynamic_update_slice | solution.py:47
  290.4 6.0 %dynamic_update_slice.46 = f32[32,16,2048]{2,1,0:T(8,128)} dynamic-update-slice(f32[32,16,2048]{2,1,0:T(8,128)} %get-tuple-element.742, f32[32,1,2048]{2,1,0:T(1,128)S(1)} %get-tuple-element.747, s32[]{:T(128)} %constant.122.clone.1..sunk.4, s32[]{:T(128)} %get-tuple-element.738, s32[]{:T(128)} %constant.122.clone.1..sunk.4) | dynamic-update-slice | bytes 524292 | tf_op jit(solution)/shard_map/while/body/eval_jaxpr/dynamic_update_slice | solution.py:47
  296.6 15.8 %while.68 = (s32[]{:T(128)}, f32[2048]{0:T(1024)S(1)}, f32[2048]{0:T(1024)S(1)}, f32[32,2048]{1,0:T(8,128)S(1)}, f32[32,2048]{1,0:T(8,128)S(1)}, /*index=5*/f32[32,2048]{1,0:T(8,128)S(1)}, f32[32,2048]{1,0:T(8,128)S(1)}) while((s32[]{:T(128)}, f32[2048]{0:T(1024)S(1)}, f32[2048]{0:T(1024)S(1)}, ...), condition=%wide.region_3.4_spmd.clone.clone, body=%wide.region_2.3_spmd.clone.sunk.clone | while | flops 10243 | bytes 131171 | solution.py:62
  312.5 8.8 %multiply_add_fusion.2 = (f32[32,16,2048]{2,1,0:T(8,128)}, f32[32,16,2048]{2,1,0:T(8,128)}) fusion(f32[32,16,2048]{2,1,0:T(8,128)} %get-tuple-element.300, f32[32,16,2048]{2,1,0:T(8,128)} %get-tuple-element.301, f32[32,2048]{1,0:T(8,128)S(1)} %get-tuple-element.304, f32[32,2048]{1,0:T(8,128)S(1)} %get-tuple-element.305), kind=kLoop, calls=%fused_computation.42 | loop fusion | flops 3145728 | bytes 17301504 | tf_op jit(solution)/shard_map/add | solution.py:64
  321.3 45.1 %while.65 = (s32[]{:T(128)}, f32[2048]{0:T(1024)S(1)}, f32[2048]{0:T(1024)S(1)}, f32[2048]{0:T(1024)S(1)}) while((s32[]{:T(128)}, f32[2048]{0:T(1024)S(1)}, f32[2048]{0:T(1024)S(1)}, f32[2048]{0:T(1024)S(1)}) %tuple.141), condition=%wide.region_5.6_spmd.clone, body=%wide.region_4.5_spmd.sunk.clone | while | flops 4098 | bytes 65629 | solution.py:150
  373.5 6.3 %all-reduce.2 = bf16[512,512]{1,0:T(8,128)(2,1)S(1)} all-reduce(f32[512,512]{1,0:T(8,128)S(1)} %fusion.37), channel_id=1, replica_groups=mesh['groups'=2,'tm'=8,'mp'=2] {'mp'}, use_global_device_ids=true, to_apply=%region_6.7 | all-reduce | flops 262144 | bytes 1572864 | tf_op jit(solution)/shard_map/psum | solution.py:157
  388.0 9.4 %collective-permute-done.2 = bf16[512,512]{1,0:T(8,128)(2,1)S(1)} collective-permute-done((bf16[512,512]{1,0:T(8,128)(2,1)S(1)}, bf16[512,512]{1,0:T(8,128)(2,1)S(1)}, u32[]{:S(2)}, u32[]{:S(2)}) %collective-permute-start.2) | collective-permute-done | bytes 524320 | tf_op jit(solution)/shard_map/ppermute | solution.py:17
  397.4 10.5 %collective-permute-done.3 = bf16[512,512]{1,0:T(8,128)(2,1)S(1)} collective-permute-done((bf16[512,512]{1,0:T(8,128)(2,1)S(1)}, bf16[512,512]{1,0:T(8,128)(2,1)S(1)}, u32[]{:S(2)}, u32[]{:S(2)}) %collective-permute-start.3) | collective-permute-done | bytes 524320 | tf_op jit(solution)/shard_map/ppermute | solution.py:17
  407.9 22.6 %collective-permute-done.4 = bf16[512,512]{1,0:T(8,128)(2,1)S(1)} collective-permute-done((bf16[512,512]{1,0:T(8,128)(2,1)S(1)}, bf16[512,512]{1,0:T(8,128)(2,1)S(1)}, u32[]{:S(2)}, u32[]{:S(2)}) %collective-permute-start.4) | collective-permute-done | bytes 524320 | tf_op jit(solution)/shard_map/ppermute | solution.py:17
  430.6 21.1 %collective-permute-done.5 = bf16[512,512]{1,0:T(8,128)(2,1)S(1)} collective-permute-done((bf16[512,512]{1,0:T(8,128)(2,1)S(1)}, bf16[512,512]{1,0:T(8,128)(2,1)S(1)}, u32[]{:S(2)}, u32[]{:S(2)}) %collective-permute-start.5) | collective-permute-done | bytes 524320 | tf_op jit(solution)/shard_map/ppermute | solution.py:17
  453.2 66.9 %while.66 = (s32[]{:T(128)}, bf16[512,2048]{1,0:T(8,128)(2,1)S(1)}, bf16[512,2048]{1,0:T(8,128)(2,1)}, bf16[2560,256]{1,0:T(8,128)(2,1)}, bf16[2560,256]{1,0:T(8...) while((s32[]{:T(128)}, bf16[512,2048]{1,0:T(8,128)(2,1)S(1)}, ...), condition=%wide.region_10.11_spmd.clone.clone, body=%wide.region_7.10_spmd.clone.sunk.clone | while | flops 1379007488 | bytes 18962580 | solution.py:176
  (275 shorter events, 355.2 us)
Async XLA Ops:
  0.6 10.0 %copy-start.4 = (bf16[2048,512]{1,0:T(8,128)(2,1)S(1)}, bf16[2048,512]{1,0:T(8,128)(2,1)}, u32[]{:S(2)}) copy-start(bf16[2048,512]{1,0:T(8,128)(2,1)} %param.29) | copy-start | bytes 6291460
  0.6 10.0 %copy-start.9 = (f32[16,512]{1,0:T(8,128)S(1)}, f32[16,512]{1,0:T(8,128)}, u32[]{:S(2)}) copy-start(f32[16,512]{1,0:T(8,128)} %param.30) | copy-start | bytes 98308
  1.6 10.8 %collective-permute-start.1 = (bf16[3,2048]{1,0:T(4,128)(2,1)S(1)}, bf16[3,2048]{1,0:T(4,128)(2,1)S(1)}, u32[]{:S(2)}, u32[]{:S(2)}) collective-permute-start(bf16[3,2048]{1,0:T(4,128)(2,1)S(1)} %slice.60), channel_id=1, source_target_pairs={{0,2},{2,4},{4,6},{6,8},{8,10},{10,12},{12,14},{1,3},{3,5},{5,7},{... | collective-permute-start | bytes 36872 | tf_op jit(solution)/shard_map/ppermute | solution.py:17
  8.4 3.9 copy-start.2
  8.5 3.9 copy-start.10
  42.7 6.1 %copy-start = (f32[512,2048]{1,0:T(8,128)S(1)}, f32[512,2048]{1,0:T(8,128)}, u32[]{:S(2)}) copy-start(f32[512,2048]{1,0:T(8,128)} %copy.23) | copy-start | bytes 12582916
  42.7 6.1 %copy-start.1 = (f32[512,2048]{1,0:T(8,128)S(1)}, f32[512,2048]{1,0:T(8,128)}, u32[]{:S(2)}) copy-start(f32[512,2048]{1,0:T(8,128)} %copy.22) | copy-start | bytes 12582916
  312.5 53.9 %copy-start.6 = (bf16[512,2048]{1,0:T(8,128)(2,1)S(1)}, bf16[512,2048]{1,0:T(8,128)(2,1)}, u32[]{:S(2)}) copy-start(bf16[512,2048]{1,0:T(8,128)(2,1)} %param.21) | copy-start | bytes 6291460
  321.3 6.4 %collective-permute-start = (f32[2048]{0:T(1024)S(1)}, f32[2048]{0:T(1024)S(1)}, u32[]{:S(2)}, u32[]{:S(2)}) collective-permute-start(f32[2048]{0:T(1024)S(1)} %multiply_add_fusion.7), channel_id=1, source_target_pairs={{0,2},{2,4},{4,6},{6,8},{8,10},{10,12},{12,14},{1,3},{3,5},{5,7},{... | collective-permute-start | bytes 24584 | tf_op jit(solution)/shard_map/while/body/eval_jaxpr/ppermute | solution.py:17
  327.7 6.4 %collective-permute-start = (f32[2048]{0:T(1024)S(1)}, f32[2048]{0:T(1024)S(1)}, u32[]{:S(2)}, u32[]{:S(2)}) collective-permute-start(f32[2048]{0:T(1024)S(1)} %multiply_add_fusion.7), channel_id=1, source_target_pairs={{0,2},{2,4},{4,6},{6,8},{8,10},{10,12},{12,14},{1,3},{3,5},{5,7},{... | collective-permute-start | bytes 24584 | tf_op jit(solution)/shard_map/while/body/eval_jaxpr/ppermute | solution.py:17
  334.2 6.4 %collective-permute-start = (f32[2048]{0:T(1024)S(1)}, f32[2048]{0:T(1024)S(1)}, u32[]{:S(2)}, u32[]{:S(2)}) collective-permute-start(f32[2048]{0:T(1024)S(1)} %multiply_add_fusion.7), channel_id=1, source_target_pairs={{0,2},{2,4},{4,6},{6,8},{8,10},{10,12},{12,14},{1,3},{3,5},{5,7},{... | collective-permute-start | bytes 24584 | tf_op jit(solution)/shard_map/while/body/eval_jaxpr/ppermute | solution.py:17
  340.6 6.4 %collective-permute-start = (f32[2048]{0:T(1024)S(1)}, f32[2048]{0:T(1024)S(1)}, u32[]{:S(2)}, u32[]{:S(2)}) collective-permute-start(f32[2048]{0:T(1024)S(1)} %multiply_add_fusion.7), channel_id=1, source_target_pairs={{0,2},{2,4},{4,6},{6,8},{8,10},{10,12},{12,14},{1,3},{3,5},{5,7},{... | collective-permute-start | bytes 24584 | tf_op jit(solution)/shard_map/while/body/eval_jaxpr/ppermute | solution.py:17
  347.1 6.4 %collective-permute-start = (f32[2048]{0:T(1024)S(1)}, f32[2048]{0:T(1024)S(1)}, u32[]{:S(2)}, u32[]{:S(2)}) collective-permute-start(f32[2048]{0:T(1024)S(1)} %multiply_add_fusion.7), channel_id=1, source_target_pairs={{0,2},{2,4},{4,6},{6,8},{8,10},{10,12},{12,14},{1,3},{3,5},{5,7},{... | collective-permute-start | bytes 24584 | tf_op jit(solution)/shard_map/while/body/eval_jaxpr/ppermute | solution.py:17
  353.5 6.4 %collective-permute-start = (f32[2048]{0:T(1024)S(1)}, f32[2048]{0:T(1024)S(1)}, u32[]{:S(2)}, u32[]{:S(2)}) collective-permute-start(f32[2048]{0:T(1024)S(1)} %multiply_add_fusion.7), channel_id=1, source_target_pairs={{0,2},{2,4},{4,6},{6,8},{8,10},{10,12},{12,14},{1,3},{3,5},{5,7},{... | collective-permute-start | bytes 24584 | tf_op jit(solution)/shard_map/while/body/eval_jaxpr/ppermute | solution.py:17
  359.9 6.4 %collective-permute-start = (f32[2048]{0:T(1024)S(1)}, f32[2048]{0:T(1024)S(1)}, u32[]{:S(2)}, u32[]{:S(2)}) collective-permute-start(f32[2048]{0:T(1024)S(1)} %multiply_add_fusion.7), channel_id=1, source_target_pairs={{0,2},{2,4},{4,6},{6,8},{8,10},{10,12},{12,14},{1,3},{3,5},{5,7},{... | collective-permute-start | bytes 24584 | tf_op jit(solution)/shard_map/while/body/eval_jaxpr/ppermute | solution.py:17
  366.4 5.9 %copy-start.5 = (bf16[2048,512]{1,0:T(8,128)(2,1)S(1)}, bf16[2048,512]{1,0:T(8,128)(2,1)}, u32[]{:S(2)}) copy-start(bf16[2048,512]{1,0:T(8,128)(2,1)} %fusion.22) | copy-start | bytes 6291460
  370.9 1.3 copy-start.7
  372.2 15.7 %copy-start.8 = (s32[4096]{0:T(1024)S(1)}, s32[4096]{0:T(1024)}, u32[]{:S(2)}) copy-start(s32[4096]{0:T(1024)} %param.31) | copy-start | bytes 49156
  379.8 17.6 %collective-permute-start.2 = (bf16[512,512]{1,0:T(8,128)(2,1)S(1)}, bf16[512,512]{1,0:T(8,128)(2,1)S(1)}, u32[]{:S(2)}, u32[]{:S(2)}) collective-permute-start(bf16[512,512]{1,0:T(8,128)(2,1)S(1)} %all-reduce.2), channel_id=1, source_target_pairs={{0,8},{2,10},{4,12},{6,14},{1,9},{3,11},{5,13},{7,15},{16,24},{18,... | collective-permute-start | bytes 1572872 | tf_op jit(solution)/shard_map/ppermute | solution.py:17
  381.1 26.8 %collective-permute-start.3 = (bf16[512,512]{1,0:T(8,128)(2,1)S(1)}, bf16[512,512]{1,0:T(8,128)(2,1)S(1)}, u32[]{:S(2)}, u32[]{:S(2)}) collective-permute-start(bf16[512,512]{1,0:T(8,128)(2,1)S(1)} %all-reduce.2), channel_id=1, source_target_pairs={{0,6},{2,8},{4,10},{6,12},{8,14},{1,7},{3,9},{5,11},{7,13},{9,15},... | collective-permute-start | bytes 1572872 | tf_op jit(solution)/shard_map/ppermute | solution.py:17
  383.1 47.4 %collective-permute-start.4 = (bf16[512,512]{1,0:T(8,128)(2,1)S(1)}, bf16[512,512]{1,0:T(8,128)(2,1)S(1)}, u32[]{:S(2)}, u32[]{:S(2)}) collective-permute-start(bf16[512,512]{1,0:T(8,128)(2,1)S(1)} %all-reduce.2), channel_id=1, source_target_pairs={{0,4},{2,6},{4,8},{6,10},{8,12},{10,14},{1,5},{3,7},{5,9},{7,11},{... | collective-permute-start | bytes 1572872 | tf_op jit(solution)/shard_map/ppermute | solution.py:17
  385.9 65.8 %collective-permute-start.5 = (bf16[512,512]{1,0:T(8,128)(2,1)S(1)}, bf16[512,512]{1,0:T(8,128)(2,1)S(1)}, u32[]{:S(2)}, u32[]{:S(2)}) collective-permute-start(bf16[512,512]{1,0:T(8,128)(2,1)S(1)} %all-reduce.2), channel_id=1, source_target_pairs={{0,2},{2,4},{4,6},{6,8},{8,10},{10,12},{12,14},{1,3},{3,5},{5,7},{... | collective-permute-start | bytes 1572872 | tf_op jit(solution)/shard_map/ppermute | solution.py:17
  520.1 1.3 copy-start.3
where the time goes:
time: 527 us; the launch traced here: 521 us
  local copies, waits for them, and re-layouts  240 us (46%)
  other arithmetic  102 us (19%)
  waiting for transfers between devices  93 us (18%)
  matrix products  50.2 us (10%)
  starting transfers between devices  26.9 us (5%)
  blocking collectives  6.27 us (1%)
    dynamic_update_slice x16, local copies, waits for them, and re-layouts, within(): lax.dynamic_update_slice_in_dim(state_buffer, run_state, row_index, 1)  96.4 us
    dynamic_update_slice x16, local copies, waits for them, and re-layouts, within(): lax.dynamic_update_slice_in_dim(prod_buffer, run_prod, row_index, 1)  96.1 us
    ppermute x12, waiting for transfers between devices, from_behind(): return lax.ppermute(block, axis, route)  93 us
    add x16, other arithmetic, within(): run_state = decay_row * run_state + input_row  49 us
    dot_general x8, matrix products, attend_block(): jnp.einsum('td,sd->ts', query_block, key_block, preferred_element_type=jn...  27.2 us
    ppermute x12, starting transfers between devices, from_behind(): return lax.ppermute(block, axis, route)  26.9 us
    dot_general x8, matrix products, attend_block(): jnp.dot(weights, value_block, preferred_element_type=jnp.float32)  20.3 us
    reduce_sum x8, other arithmetic, attend_block(): totals = jnp.sum(weights_raw, axis=-1, keepdims=True)  19.1 us
  transfers between devices with their start and end apart: 12, of which 11 were waited for; matrix products, arithmetic and copies ran while one was open for 1% of the time, Pallas kernels for 0%

commit v1 on v0

v1 whole, which is shorter than its diff:
```python
import functools

import jax
import jax.numpy as jnp
from jax import lax
from jax.experimental import pallas as pl
from jax.experimental.pallas import tpu as pltpu
from jax.sharding import PartitionSpec as P

HD = 256
CONV = 4
WINDOW = 2048
SCALE_ROWS = 128
RUNS = 8
TILE = 256
MESH = pl.DeviceIdType.MESH


def sigmoid(x):
    return 0.5 + 0.5 * jnp.tanh(0.5 * x)


def gelu(x):
    return 0.5 * x * (1.0 + jnp.tanh(0.7978845608028654 * (x + 0.044715 * (x * x * x))))


def expm1_small(x):
    p = 1.0 / 5040.0
    for c in (1.0 / 720.0, 1.0 / 120.0, 1.0 / 24.0, 1.0 / 6.0, 0.5, 1.0):
        p = p * x + c
    return p * x


def scaled(panel, scale_lo, scale_hi):
    lo = panel[:SCALE_ROWS].astype(jnp.float32) * scale_lo
    hi = panel[SCALE_ROWS:].astype(jnp.float32) * scale_hi
    return jnp.concatenate([lo, hi], 0).astype(jnp.bfloat16)


def recur_kernel(
    n, x_hbm, y_hbm, gp_hbm, kvp_hbm, cw_ref, cb_ref, gs_ref, gb_ref, rate_ref, kvs_ref, masks_ref,
    mixed_hbm, kv_hbm,
    xv, yv, gpv, kvpv, xs, g, convb, pbuf, sbuf, gel, perm, unperm, halo, summ, gath, inc8,
    kvacc, kvrecv, kvbuf, mixv,
    load_sem, halo_sem, st_send, st_recv, kvx_sem, fwd_send, fwd_recv, pt_send, pt_recv, out_sem,
):
    me = lax.axis_index("tm")
    half = lax.axis_index("mp")
    T, C = xv.shape
    nb = C // HD
    steps = T // RUNS

    loads = [
        pltpu.make_async_copy(s, d, load_sem.at[i])
        for i, (s, d) in enumerate(((x_hbm, xv), (gp_hbm, gpv), (y_hbm, yv), (kvp_hbm, kvpv)))
    ]
    for c in loads:
        c.start()

    barrier = pltpu.get_barrier_semaphore()
    for k in range(1, n):
        pl.semaphore_signal(
            barrier, inc=1, device_id={"tm": lax.rem(me + k, n)}, device_id_type=MESH
        )
    pl.semaphore_signal(barrier, inc=1, device_id={"mp": 1 - half}, device_id_type=MESH)

    row = lax.broadcasted_iota(jnp.int32, (T, T), 0)
    col = lax.broadcasted_iota(jnp.int32, (T, T), 1)
    sh = steps.bit_length() - 1
    at_row = lax.bitwise_and(row, RUNS - 1) * steps + lax.shift_right_logical(row, 3)
    perm[...] = (at_row == col).astype(jnp.float32).astype(jnp.bfloat16)
    at_col = lax.bitwise_and(col, RUNS - 1) * steps + lax.shift_right_logical(col, 3)
    unperm[...] = (at_col == row).astype(jnp.float32).astype(jnp.bfloat16)

    pl.semaphore_wait(barrier, n)
    halo_copy = pltpu.make_async_remote_copy(
        src_ref=x_hbm.at[pl.ds(T - 16, 16), :], dst_ref=halo,
        send_sem=halo_sem.at[0], recv_sem=halo_sem.at[1],
        device_id={"tm": lax.rem(me + 1, n)}, device_id_type=MESH,
    )

    @pl.when(me < n - 1)
    def _():
        halo_copy.start()

    @pl.when(me == 0)
    def _():
        halo[...] = jnp.zeros_like(halo)

    loads[0].wait()

    @pl.when(me > 0)
    def _():
        halo_copy.wait_recv()

    loads[1].wait()

    def block(b, _):
        cs = pl.ds(pl.multiple_of(b * HD, HD), HD)
        xp = jnp.dot(perm[...], xv[:, cs], preferred_element_type=jnp.float32)
        xs[pl.ds(24, T), :] = xp
        first = lax.broadcasted_iota(jnp.int32, (RUNS, HD), 0) == 0
        halo_f = halo[:, cs].astype(jnp.float32)
        for j in range(1, CONV):
            tail = xs[pl.ds(24 + T - 8 * j, 8), :]
            rolled = pltpu.roll(tail, 1, 0)
            xs[pl.ds(24 - 8 * j, 8), :] = jnp.where(first, halo_f[16 - j:17 - j], rolled)
        bias = cb_ref[:, cs]
        taps = [cw_ref[pl.ds(j, 1), cs] for j in range(CONV)]

        def conv_rows(i, _):
            r0 = pl.multiple_of(i * 64, 64)
            total = taps[0] * xs[pl.ds(r0 + 24, 64), :]
            for j in range(1, CONV):
                same = masks_ref[pl.ds(r0, 64), j - 1:j]
                total = total + taps[j] * (xs[pl.ds(r0 + 24 - 8 * j, 64), :] * same)
            convb[pl.ds(r0, 64), :] = (total + bias).astype(jnp.bfloat16)
            return 0

        lax.fori_loop(0, T // 64, conv_rows, 0)
        scales = gs_ref[b]
        gw = scaled(gpv[b], scales[0:1], scales[1:2])
        g[...] = jnp.dot(convb[...], gw, preferred_element_type=jnp.float32)
        b0, b1 = gb_ref[0:1, cs], gb_ref[1:2, cs]
        rate = -8.0 * rate_ref[:, cs]

        def rows(i, carry):
            prod, state = carry
            r0 = pl.multiple_of(i * 32, 32)
            rs = pl.ds(r0, 32)
            recur = sigmoid(g[rs, :HD] + b0)
            gate = sigmoid(g[rs, HD:] + b1)
            keep = masks_ref[rs, 0:1]
            e = expm1_small(recur * rate)
            a = (1.0 + e) * keep
            q = -e * (2.0 + e)
            m = q * lax.rsqrt(jnp.maximum(q, 1e-37))
            m = 1.0 + keep * (m - 1.0)
            u = gate * convb[rs, :].astype(jnp.float32) * m
            for k in range(4):
                ak = a[8 * k:8 * k + 8]
                prod = ak * prod
                state = ak * state + u[8 * k:8 * k + 8]
                pbuf[pl.ds(r0 + 8 * k, 8), cs] = prod
                sbuf[pl.ds(r0 + 8 * k, 8), cs] = state
            return prod, state

        lax.fori_loop(
            0, T // 32, rows, (jnp.ones((RUNS, HD), jnp.float32), jnp.zeros((RUNS, HD), jnp.float32))
        )
        return 0

    lax.fori_loop(0, nb, block, 0)

    p_end = pbuf[pl.ds(T - 8, 8), :]
    s_end = sbuf[pl.ds(T - 8, 8), :]
    dp, ds = p_end[0:1], s_end[0:1]
    for s in range(1, RUNS):
        ds = p_end[s:s + 1] * ds + s_end[s:s + 1]
        dp = p_end[s:s + 1] * dp
    summ[0:1, :] = dp
    summ[1:2, :] = ds

    def state_copy(k):
        return pltpu.make_async_remote_copy(
            src_ref=summ, dst_ref=gath.at[k], send_sem=st_send.at[k], recv_sem=st_recv.at[k],
            device_id={"tm": lax.rem(me + k, n)}, device_id_type=MESH,
        )

    for k in range(1, n):
        @pl.when(me + k < n)
        def _(k=k):
            state_copy(k).start()

    loads[2].wait()

    def gelu_block(b, _):
        cs = pl.ds(pl.multiple_of(b * HD, HD), HD)
        gel[:, cs] = gelu(jnp.dot(perm[...], yv[:, cs], preferred_element_type=jnp.float32))
        return 0

    lax.fori_loop(0, nb, gelu_block, 0)
    loads[3].wait()

    inc8[0:1, :] = jnp.zeros((1, C), jnp.float32)
    for k in range(n - 1, 0, -1):
        @pl.when(me >= k)
        def _(k=k):
            state_copy(k).wait_recv()
            inc8[0:1, :] = gath[k, 0:1, :] * inc8[0:1, :] + gath[k, 1:2, :]
    cur = inc8[0:1, :]
    for s in range(RUNS - 1):
        cur = p_end[s:s + 1] * cur + s_end[s:s + 1]
        inc8[s + 1:s + 2, :] = cur

    kvacc[...] = jnp.zeros_like(kvacc)

    def mix_block(b, _):
        cs = pl.ds(pl.multiple_of(b * HD, HD), HD)
        entering = jnp.concatenate([inc8[:, cs]] * 8, 0)

        def mix_rows(i, _):
            rs = pl.ds(pl.multiple_of(i * 64, 64), 64)
            state = sbuf[rs, cs] + pbuf[rs, cs] * entering
            convb[rs, :] = (state * gel[rs, cs]).astype(jnp.bfloat16)
            return 0

        lax.fori_loop(0, T // 64, mix_rows, 0)
        mixed = jnp.dot(
            unperm[...], convb[...], preferred_element_type=jnp.float32
        ).astype(jnp.bfloat16)
        mixv[:, cs] = mixed
        kw = scaled(
            kvpv[pl.ds(pl.multiple_of(b * HD, HD), HD), :],
            kvs_ref[pl.ds(2 * b, 1), :], kvs_ref[pl.ds(2 * b + 1, 1), :],
        )
        kvacc[...] += jnp.dot(mixed, kw, preferred_element_type=jnp.float32)
        return 0

    lax.fori_loop(0, nb, mix_block, 0)
    mixed_out = pltpu.make_async_copy(mixv, mixed_hbm, out_sem.at[0])
    mixed_out.start()

    own_cols = pl.ds(pl.multiple_of(half * HD, HD), HD)
    their_cols = pl.ds(pl.multiple_of((1 - half) * HD, HD), HD)
    partner = {"mp": 1 - half}
    exchange = pltpu.make_async_remote_copy(
        src_ref=kvacc.at[:, their_cols], dst_ref=kvrecv,
        send_sem=kvx_sem.at[0], recv_sem=kvx_sem.at[1], device_id=partner, device_id_type=MESH,
    )
    exchange.start()
    exchange.wait_recv()
    kvbuf[0, half] = (kvacc[:, own_cols] + kvrecv[...]).astype(jnp.bfloat16)

    odd = lax.rem(me, 2) == 1
    even = lax.rem(me, 2) == 0

    def forward(src, dst, sem, to):
        return pltpu.make_async_remote_copy(
            src_ref=kvbuf.at[src, half], dst_ref=kvbuf.at[dst, half],
            send_sem=fwd_send.at[sem], recv_sem=fwd_recv.at[dst],
            device_id={"tm": lax.rem(me + to + n, n)}, device_id_type=MESH,
        )

    def share(slot):
        return pltpu.make_async_remote_copy(
            src_ref=kvbuf.at[slot, half], dst_ref=kvbuf.at[slot, half],
            send_sem=pt_send.at[slot], recv_sem=pt_recv.at[slot],
            device_id=partner, device_id_type=MESH,
        )

    def arrived(slot):
        forward(0, slot, 0, 2).wait_recv()

    z_first, z_second = forward(0, 2, 0, 2), forward(2, 4, 1, 2)
    even_a, even_b = forward(0, 1, 2, 1), forward(2, 3, 3, 1)
    odd_a, odd_b = forward(2, 1, 2, -1), forward(4, 3, 3, -1)
    ahead = me + 2 < n

    def when(cond, do):
        pl.when(cond)(do)

    when(ahead, z_first.start)
    when(even, even_a.start)
    share(0).start()

    @pl.when(me >= 2)
    def _():
        arrived(2)
        when(ahead, z_second.start)
        when(even, even_b.start)
        when(odd, odd_a.start)
        share(2).start()

    @pl.when(me >= 1)
    def _():
        arrived(1)
        share(1).start()

    @pl.when(me >= 4)
    def _():
        arrived(4)
        when(odd, odd_b.start)
        share(4).start()

    @pl.when(me >= 3)
    def _():
        arrived(3)
        share(3).start()

    outs = [pltpu.make_async_copy(kvbuf.at[k], kv_hbm.at[4 - k], out_sem.at[1 + k]) for k in range(5)]
    for k in range(5):
        @pl.when(me >= k)
        def _(k=k):
            share(k).wait()
            outs[k].start()

    for k in range(1, n):
        @pl.when(me + k < n)
        def _(k=k):
            state_copy(k).wait_send()

    @pl.when(me < n - 1)
    def _():
        halo_copy.wait_send()

    exchange.wait_send()
    when(ahead, z_first.wait_send)
    when(even, even_a.wait_send)

    @pl.when(me >= 2)
    def _():
        when(ahead, z_second.wait_send)
        when(even, even_b.wait_send)
        when(odd, odd_a.wait_send)

    when(odd & (me >= 4), odd_b.wait_send)
    for k in range(5):
        when(me >= k, outs[k].wait)
    mixed_out.wait()


def attend_kernel(lo_ref, q_ref, kv_ref, qid_ref, kid_ref, mixed_in, o_ref, mixed_out, bias, scores, acc, top, low, sem):
    j = pl.program_id(0)
    heads = q_ref.shape[1] // HD
    pass_on = pltpu.make_async_copy(mixed_in, mixed_out, sem)

    @pl.when(j == 0)
    def _():
        pass_on.start()

    lo = lo_ref[j]
    hi = WINDOW // TILE + j + 1
    per = kv_ref.shape[2] // TILE
    c = HD ** (-0.5) * 1.4426950408889634
    qid = qid_ref[...]
    offset = lax.broadcasted_iota(jnp.int32, (TILE, TILE), 0) - lax.broadcasted_iota(
        jnp.int32, (TILE, TILE), 1
    )
    top[...] = jnp.full_like(top, -3e38)
    low[...] = jnp.zeros_like(low)
    acc[...] = jnp.zeros_like(acc)

    def score(t, _):
        blk, r = t // per, lax.rem(t, per)
        keys = kv_ref[blk, 0, pl.ds(pl.multiple_of(r * TILE, TILE), TILE), :]
        back = offset + (WINDOW + (j - t) * TILE)
        ok = (back >= 0) & (back < WINDOW) & (kid_ref[t] == qid)
        bias[...] = jnp.where(ok, 0.0, -1e30)
        for h in range(heads):
            s = lax.dot_general(
                q_ref[:, h * HD:(h + 1) * HD], keys, (((1,), (1,)), ((), ())),
                preferred_element_type=jnp.float32,
            ) + bias[...]
            scores[h, t] = s
            top[h] = jnp.maximum(top[h], jnp.maximum(s[:, :128], s[:, 128:]))
        return 0

    lax.fori_loop(lo, hi, score, 0)
    for h in range(heads):
        top[h] = jnp.broadcast_to(jnp.max(top[h], axis=1, keepdims=True), (TILE, 128))

    def weigh(t, _):
        blk, r = t // per, lax.rem(t, per)
        values = kv_ref[blk, 1, pl.ds(pl.multiple_of(r * TILE, TILE), TILE), :]
        for h in range(heads):
            m = top[h]
            s = scores[h, t]
            w = [jnp.exp2((s[:, i * 128:(i + 1) * 128] - m) * c) for i in range(2)]
            low[h] += w[0] + w[1]
            acc[h] += jnp.dot(
                jnp.concatenate(w, 1).astype(jnp.bfloat16), values, preferred_element_type=jnp.float32
            )
        return 0

    lax.fori_loop(lo, hi, weigh, 0)
    for h in range(heads):
        total = jnp.sum(low[h], axis=1, keepdims=True)
        o_ref[:, h * HD:(h + 1) * HD] = (acc[h] * (1.0 / total)).astype(jnp.bfloat16)

    @pl.when(j == pl.num_programs(0) - 1)
    def _():
        pass_on.wait()


def local(
    n, branch_x, branch_y, queries, conv_weight, conv_bias, gate_panel, gate_scale, gate_bias,
    decay_rate, kv_panel, kv_scale, segment_ids,
):
    T, C = branch_x.shape
    f32, bf16 = jnp.float32, jnp.bfloat16
    heads = queries.shape[1] // HD
    first_row = lax.axis_index("tm") * T
    padded_ids = jnp.concatenate([-jnp.ones((WINDOW,), jnp.int32), segment_ids])
    key_ids = lax.dynamic_slice_in_dim(padded_ids, first_row, WINDOW + T)
    own_ids = key_ids[WINDOW:]
    masks = jnp.stack(
        [(key_ids[WINDOW - j:WINDOW - j + T] == own_ids).astype(f32) for j in range(1, CONV)], -1
    )
    masks = masks.reshape(RUNS, T // RUNS, CONV - 1).transpose(1, 0, 2).reshape(T, CONV - 1)
    vmem, anyw = pl.BlockSpec(memory_space=pltpu.VMEM), pl.BlockSpec(memory_space=pl.ANY)
    dma = pltpu.SemaphoreType.DMA
    mixed, kv = pl.pallas_call(
        functools.partial(recur_kernel, n),
        out_shape=(
            jax.ShapeDtypeStruct((T, C), bf16), jax.ShapeDtypeStruct((5, 2, T, HD), bf16),
        ),
        in_specs=[anyw] * 4 + [vmem] * 7,
        out_specs=(anyw, anyw),
        scratch_shapes=[
            pltpu.VMEM((T, C), bf16), pltpu.VMEM((T, C), bf16),
            pltpu.VMEM(gate_panel.shape, bf16), pltpu.VMEM(kv_panel.shape, bf16),
            pltpu.VMEM((T + 24, HD), f32), pltpu.VMEM((T, 2 * HD), f32), pltpu.VMEM((T, HD), bf16),
            pltpu.VMEM((T, C), f32), pltpu.VMEM((T, C), f32), pltpu.VMEM((T, C), f32),
            pltpu.VMEM((T, T), bf16), pltpu.VMEM((T, T), bf16), pltpu.VMEM((16, C), bf16),
            pltpu.VMEM((2, C), f32), pltpu.VMEM((n, 2, C), f32), pltpu.VMEM((RUNS, C), f32),
            pltpu.VMEM((T, 2 * HD), f32), pltpu.VMEM((T, HD), f32),
            pltpu.VMEM((5, 2, T, HD), bf16), pltpu.VMEM((T, C), bf16),
            dma((4,)), dma((2,)), dma((n,)), dma((n,)), dma((2,)), dma((4,)), dma((5,)),
            dma((5,)), dma((5,)), dma((6,)),
        ],
        compiler_params=pltpu.CompilerParams(
            collective_id=0, has_side_effects=True, vmem_limit_bytes=56 * 1024 * 1024
        ),
        name="recurrence",
    )(
        branch_x, branch_y, gate_panel, kv_panel, conv_weight, conv_bias[None], gate_scale,
        gate_bias, decay_rate[None], kv_scale, masks,
    )
    tiles = (WINDOW + T) // TILE
    row0 = jnp.arange(T // TILE, dtype=jnp.int32) * TILE
    doc = jnp.sum((key_ids[None, :] < own_ids[::TILE][:, None]).astype(jnp.int32), 1)
    lo = jnp.maximum(doc, row0 + 1) // TILE
    attended, mixed = pl.pallas_call(
        attend_kernel,
        out_shape=(
            jax.ShapeDtypeStruct(queries.shape, bf16), jax.ShapeDtypeStruct((T, C), bf16),
        ),
        grid_spec=pltpu.PrefetchScalarGridSpec(
            num_scalar_prefetch=1,
            grid=(T // TILE,),
            in_specs=[
                pl.BlockSpec((TILE, heads * HD), lambda j, lo: (j, 0)),
                pl.BlockSpec(memory_space=pltpu.VMEM),
                pl.BlockSpec((TILE, 1), lambda j, lo: (j, 0)),
                pl.BlockSpec(memory_space=pltpu.VMEM),
                anyw,
            ],
            out_specs=(pl.BlockSpec((TILE, heads * HD), lambda j, lo: (j, 0)), anyw),
            scratch_shapes=[
                pltpu.VMEM((TILE, TILE), f32), pltpu.VMEM((heads, tiles, TILE, TILE), f32),
                pltpu.VMEM((heads, TILE, HD), f32), pltpu.VMEM((heads, TILE, 128), f32),
                pltpu.VMEM((heads, TILE, 128), f32), dma,
            ],
        ),
        compiler_params=pltpu.CompilerParams(vmem_limit_bytes=56 * 1024 * 1024),
        name="attention",
    )(lo, queries, kv, own_ids[:, None], key_ids.reshape(tiles, 1, TILE), mixed)
    return (mixed, attended)


def solution(mesh):
    rows = P(("groups", "tm"), "mp")
    in_specs = (
        rows, rows, rows, P(None, "mp"), P("mp"), P("mp", None, None), P("mp", None, None),
        P(None, "mp"), P("mp"), P("mp", None), P("mp", None), P("groups"),
    )
    return jax.shard_map(
        functools.partial(local, mesh.shape["tm"]), mesh=mesh, in_specs=in_specs,
        out_specs=(rows, rows), check_vma=False,
    )
```

time: 527 us -> 143 us (0.27)
  local copies, waits for them, and re-layouts: 240 us -> 3.47 us
  Pallas kernels: 0 us -> 135 us
  other arithmetic: 102 us -> 2.43 us
  waiting for transfers between devices: 93 us -> 0 us
  matrix products: 50.2 us -> 0 us
  starting transfers between devices: 26.9 us -> 0 us
  blocking collectives: 6.27 us -> 0 us
    dynamic_update_slice x96 -> x0, local copies, waits for them, and re-layouts: 206 us -> none  [the longest x16 96.4 us: within(): lax.dynamic_update_slice_in_dim(state_buffer, run_state, row_index, 1)]
    pallas_call x0 -> x2, Pallas kernels: none -> 135 us  [the longest x1 68.4 us: local(): pl.pallas_call(attend_kernel, out_shape=(jax.ShapeDtypeStruct(queries.sha...]
    ppermute x12 -> x0, waiting for transfers between devices: 93 us -> none  [from_behind(): return lax.ppermute(block, axis, route)]
    add x57 -> x0, other arithmetic: 58.1 us -> none  [the longest x16 49 us: within(): run_state = decay_row * run_state + input_row]
    dot_general x18 -> x0, matrix products: 50.2 us -> none  [the longest x8 27.2 us: attend_block(): jnp.einsum('td,sd->ts', query_block, key_block, preferred_element_type=jn...]
    ppermute x12 -> x0, starting transfers between devices: 26.9 us -> none  [from_behind(): return lax.ppermute(block, axis, route)]
    reduce_sum x8 -> x1, other arithmetic: 19.1 us -> 0.2 us  [local(): jnp.sum((key_ids[None, :] < own_ids[::TILE][:, None]).astype(jnp.int32), 1)]
    reshape x3 -> x2, local copies, waits for them, and re-layouts: 15.9 us -> 1.48 us  [the longest x1 0.86 us: local(): masks.reshape(RUNS, T // RUNS, CONV - 1).transpose(1, 0, 2)]
  transfers between devices with their start and end apart: 12 -> 0, of which waited for: 11 -> 0; matrix products, arithmetic and copies ran while one was open for 1% -> 0% of each run, Pallas kernels for 0% -> 0%
where the time goes in v1:
time: 143 us; the launch traced here: 142 us
  Pallas kernels  135 us (94%)
  local copies, waits for them, and re-layouts  3.47 us (2%)
  other arithmetic  2.43 us (2%)
    pallas_call x1, Pallas kernels, local(): pl.pallas_call(attend_kernel, out_shape=(jax.ShapeDtypeStruct(queries.sha...  68.4 us
    pallas_call x1, Pallas kernels, local(): pl.pallas_call(functools.partial(recur_kernel, n), out_shape=(jax.ShapeDt...  66.9 us

profile of v1, /device:TPU:16, one launch (start us, length us, event | category | flops | bytes accessed | tf_op | source)
XLA Modules:
  0.0 141.8 jit_solution(12869193862932174517)
XLA Ops:
  0.6 0.8 fusion.1
  1.5 0.9 fusion.2
  2.3 0.1 convert_element_type.32
  2.4 0.1 convert_element_type.31
  2.5 0.1 slice.34
  2.6 0.1 convert_element_type.33
  2.7 0.8 pad_dynamic-slice_fusion.4
  3.5 0.2 fusion
  3.7 0.6 reshape.89.kid_ref
  4.3 0.5 and_select_fusion.lo_ref
  4.8 0.9 copy.16
  5.7 0.9 copy.17.qid_ref
  6.5 66.9 %recurrence.1 = (bf16[512,2048]{1,0:T(8,128)(2,1)}, bf16[5,2,512,256]{3,2,1,0:T(8,128)(2,1)}) custom-call(bf16[512,2048]{1,0:T(8,128)(2,1)} %x_hbm.1, bf16[512,2048]{1,0:T(8,128)(2,1)} %y_hbm.1, bf16[8,256,512]{2,1,0:T(8,128)(2,1)} %gp_hbm.1, bf16[2048,512]{1,0:T(8,128)(2,1)} %kvp_hbm.1, f32[4,2048]{1,0:T(4,128)} %cw_ref.1, f32[1,2048]{1,0:T(1,128)} %bitcast.8, ...), custom_call_target="tpu_custom_call" | custom-call | tf_op jit(solution)/shard_map/recurrence/pallas_call | solution.py:403
  73.4 68.4 %attention.1 = (bf16[512,2048]{1,0:T(8,128)(2,1)}, bf16[512,2048]{1,0:T(8,128)(2,1)}) custom-call(s32[2]{0:T(128)} %and_select_fusion.lo_ref, bf16[512,2048]{1,0:T(8,128)(2,1)} %q_ref.1, bf16[5,2,512,256]{3,2,1,0:T(8,128)(2,1)} %get-tuple-element.6.kv_ref, s32[512,1]{1,0:T(8,128)} %copy.17.qid_ref, s32[10,1,256]{2,1,0:T(1,128)} %reshape.89.kid_ref, ...), custom_call_target="tpu_custom_call" | custom-call | tf_op jit(solution)/shard_map/attention/pallas_call | solution.py:434
  (1 shorter events, 0.0 us)

commit v2 on v1

--- a/solution.py
+++ b/solution.py
@@ -126,8 +126,8 @@
 
         def rows(i, carry):
             prod, state = carry
-            r0 = pl.multiple_of(i * 32, 32)
-            rs = pl.ds(r0, 32)
+            r0 = pl.multiple_of(i * 64, 64)
+            rs = pl.ds(r0, 64)
             recur = sigmoid(g[rs, :HD] + b0)
             gate = sigmoid(g[rs, HD:] + b1)
             keep = masks_ref[rs, 0:1]
@@ -137,7 +137,7 @@
             m = q * lax.rsqrt(jnp.maximum(q, 1e-37))
             m = 1.0 + keep * (m - 1.0)
             u = gate * convb[rs, :].astype(jnp.float32) * m
-            for k in range(4):
+            for k in range(8):
                 ak = a[8 * k:8 * k + 8]
                 prod = ak * prod
                 state = ak * state + u[8 * k:8 * k + 8]
@@ -146,7 +146,7 @@
             return prod, state
 
         lax.fori_loop(
-            0, T // 32, rows, (jnp.ones((RUNS, HD), jnp.float32), jnp.zeros((RUNS, HD), jnp.float32))
+            0, T // 64, rows, (jnp.ones((RUNS, HD), jnp.float32), jnp.zeros((RUNS, HD), jnp.float32))
         )
         return 0
 
@@ -320,15 +320,10 @@
     mixed_out.wait()
 
 
-def attend_kernel(lo_ref, q_ref, kv_ref, qid_ref, kid_ref, mixed_in, o_ref, mixed_out, bias, scores, acc, top, low, sem):
+def attend_kernel(lo_ref, q_ref, kv_ref, qid_ref, kid_ref, mixed_in, o_ref, mixed_out, bias, scores, acc, top, low):
     j = pl.program_id(0)
     heads = q_ref.shape[1] // HD
-    pass_on = pltpu.make_async_copy(mixed_in, mixed_out, sem)
-
-    @pl.when(j == 0)
-    def _():
-        pass_on.start()
-
+    mixed_out[...] = mixed_in[...]
     lo = lo_ref[j]
     hi = WINDOW // TILE + j + 1
     per = kv_ref.shape[2] // TILE
@@ -377,10 +372,6 @@
     for h in range(heads):
         total = jnp.sum(low[h], axis=1, keepdims=True)
         o_ref[:, h * HD:(h + 1) * HD] = (acc[h] * (1.0 / total)).astype(jnp.bfloat16)
-
-    @pl.when(j == pl.num_programs(0) - 1)
-    def _():
-        pass_on.wait()
 
 
 def local(
@@ -444,13 +435,16 @@
                 pl.BlockSpec(memory_space=pltpu.VMEM),
                 pl.BlockSpec((TILE, 1), lambda j, lo: (j, 0)),
                 pl.BlockSpec(memory_space=pltpu.VMEM),
-                anyw,
+                pl.BlockSpec((TILE, C), lambda j, lo: (j, 0)),
             ],
-            out_specs=(pl.BlockSpec((TILE, heads * HD), lambda j, lo: (j, 0)), anyw),
+            out_specs=(
+                pl.BlockSpec((TILE, heads * HD), lambda j, lo: (j, 0)),
+                pl.BlockSpec((TILE, C), lambda j, lo: (j, 0)),
+            ),
             scratch_shapes=[
                 pltpu.VMEM((TILE, TILE), f32), pltpu.VMEM((heads, tiles, TILE, TILE), f32),
                 pltpu.VMEM((heads, TILE, HD), f32), pltpu.VMEM((heads, TILE, 128), f32),
-                pltpu.VMEM((heads, TILE, 128), f32), dma,
+                pltpu.VMEM((heads, TILE, 128), f32),
             ],
         ),
         compiler_params=pltpu.CompilerParams(vmem_limit_bytes=56 * 1024 * 1024),

time: 143 us -> 95.1 us (0.67)
  Pallas kernels: 135 us -> 87.8 us
    pallas_call x1, Pallas kernels: 68.4 us -> 23.8 us  [local(): pl.pallas_call(attend_kernel, out_shape=(jax.ShapeDtypeStruct(queries.sha...]
    pallas_call x1, Pallas kernels: 66.9 us -> 63.9 us  [local(): pl.pallas_call(functools.partial(recur_kernel, n), out_shape=(jax.ShapeDt...]
where the time goes in v2:
time: 95.1 us; the launch traced here: 94.3 us
  Pallas kernels  87.8 us (92%)
  local copies, waits for them, and re-layouts  3.47 us (4%)
  other arithmetic  2.43 us (3%)
    pallas_call x1, Pallas kernels, local(): pl.pallas_call(functools.partial(recur_kernel, n), out_shape=(jax.ShapeDt...  63.9 us
    pallas_call x1, Pallas kernels, local(): pl.pallas_call(attend_kernel, out_shape=(jax.ShapeDtypeStruct(queries.sha...  23.8 us

profile of v2, /device:TPU:16, one launch (start us, length us, event | category | flops | bytes accessed | tf_op | source)
XLA Modules:
  0.0 94.3 jit_solution(17889251150876531203)
XLA Ops:
  0.6 0.8 fusion.1
  1.5 0.9 fusion.2
  2.3 0.1 convert_element_type.32
  2.4 0.1 convert_element_type.31
  2.5 0.1 slice.34
  2.6 0.1 convert_element_type.33
  2.7 0.8 pad_dynamic-slice_fusion.4
  3.5 0.2 fusion
  3.7 0.6 reshape.89.kid_ref
  4.3 0.5 and_select_fusion.lo_ref
  4.8 0.9 copy.16
  5.7 0.9 copy.17.qid_ref
  6.5 63.9 %recurrence.1 = (bf16[512,2048]{1,0:T(8,128)(2,1)}, bf16[5,2,512,256]{3,2,1,0:T(8,128)(2,1)}) custom-call(bf16[512,2048]{1,0:T(8,128)(2,1)} %x_hbm.1, bf16[512,2048]{1,0:T(8,128)(2,1)} %y_hbm.1, bf16[8,256,512]{2,1,0:T(8,128)(2,1)} %gp_hbm.1, bf16[2048,512]{1,0:T(8,128)(2,1)} %kvp_hbm.1, f32[4,2048]{1,0:T(4,128)} %cw_ref.1, f32[1,2048]{1,0:T(1,128)} %bitcast.8, ...), custom_call_target="tpu_custom_call" | custom-call | tf_op jit(solution)/shard_map/recurrence/pallas_call | solution.py:394
  70.5 23.8 %attention.1 = (bf16[512,2048]{1,0:T(8,128)(2,1)}, bf16[512,2048]{1,0:T(8,128)(2,1)}) custom-call(s32[2]{0:T(128)} %and_select_fusion.lo_ref, bf16[512,2048]{1,0:T(8,128)(2,1)} %q_ref.1, bf16[5,2,512,256]{3,2,1,0:T(8,128)(2,1)} %get-tuple-element.6.kv_ref, s32[512,1]{1,0:T(8,128)} %copy.17.qid_ref, s32[10,1,256]{2,1,0:T(1,128)} %reshape.89.kid_ref, ...), custom_call_target="tpu_custom_call" | custom-call | tf_op jit(solution)/shard_map/attention/pallas_call | solution.py:425
  (1 shorter events, 0.0 us)
